TPU v7x, 32 devices: a whole 2x2x4 slice. The times are simulated.
32 devices in a mesh: tp: 4 (over x, core), ep: 8 (over z, y).
Axes of the slice: x: 2, y: 2, z: 4, core: 2. Of those that a mesh axis runs over, the one named last changes fastest.
Arguments:
- tokens: bfloat16 [8192, 1024], P('ep'), may hold values from -6 to 6
- segments: int32 [8, 1024], P('ep'), may hold values from 0 to 7, never falling along the last dimension, each value on 1 to 512 neighbouring positions
- routes: int32 [8192], P('ep'), may hold values from 0 to 7, as said below
- capacity: int32 [8], replicated, may hold values from 96 to 192, as said below
- ln1_gain: float32 [1024], replicated, may hold values from 0.25 to 1.75
- ln1_bias: float32 [1024], replicated, may hold values from -1.2 to 1.2
- qkv_weight: bfloat16 [3, 1024, 1024], P(None, None, 'tp'), may hold values from -0.1875 to 0.1875
- out_weight: bfloat16 [1024, 1024], P('tp'), may hold values from -0.75 to 0.75
- ln2_gain: float32 [1024], replicated, may hold values from 0.25 to 1.75
- ln2_bias: float32 [1024], replicated, may hold values from -1.2 to 1.2
- mix_weight: bfloat16 [1024, 2], replicated, may hold values from -0.1875 to 0.1875
- up_weight: bfloat16 [1024, 4096], P(None, 'tp'), may hold values from -0.1875 to 0.1875
- down_weight: bfloat16 [4096, 1024], P('tp'), may hold values from -0.1875 to 0.1875
- expert_up: bfloat16 [8, 1024, 4096], P('ep', None, 'tp'), may hold values from -0.1875 to 0.1875
- expert_down: bfloat16 [8, 4096, 1024], P('ep', 'tp'), may hold values from -0.1875 to 0.1875
- cotangent: bfloat16 [8192, 1024], P('ep'), may hold values from -6 to 6
Outputs:
- output: bfloat16 [8192, 1024], P('ep')
- grad_tokens: bfloat16 [8192, 1024], P('ep')
- grad_ln1_gain: float32 [1024], replicated
- grad_ln1_bias: float32 [1024], replicated
- grad_qkv: float32 [3, 1024, 1024], P(None, None, 'tp')
- grad_out: float32 [1024, 1024], P('tp')
- grad_ln2_gain: float32 [1024], replicated
- grad_ln2_bias: float32 [1024], replicated
- grad_mix: float32 [1024, 2], replicated
- grad_up: float32 [1024, 4096], P(None, 'tp')
- grad_down: float32 [4096, 1024], P('tp')
- grad_expert_up: float32 [8, 1024, 4096], P('ep', None, 'tp')
- grad_expert_down: float32 [8, 4096, 1024], P('ep', 'tp')
Inputs may be any that keep to these rules, and one draw needn't show every extreme that they name: `routes`: in the tokens of each index of ep, one expert is named 192 times or more, and its capacity is 192. One expert's capacity is 192.
All inputs are finite; a program needn't handle non-finite values.
Results may differ from a plain program's by a relative error of at most 0.033.
Values may be sent and summed in bfloat16 or wider, within the bound.
A program may use at most 192 MiB of HBM per device.

v0:
```python
import math

import jax
import jax.numpy as jnp
from jax import lax
from jax.sharding import PartitionSpec as P

HD = 64


epsilon = 1e-05
masked_value = -1e30
block_limit = 512


def layer_norm(values, gain_row, bias_row):
    centred = values - jnp.mean(values, axis=-1, keepdims=True)
    spread = lax.rsqrt(jnp.mean(centred * centred, axis=-1, keepdims=True) + epsilon)
    unit_rows = centred * spread
    return (unit_rows * gain_row + bias_row, unit_rows, spread)


def norm_back(upstream, unit_rows, spread, gain_row):
    scaled = upstream * gain_row
    inner = (
        scaled
        - jnp.mean(scaled, axis=-1, keepdims=True)
        - unit_rows * jnp.mean(scaled * unit_rows, axis=-1, keepdims=True)
    )
    return (spread * inner, jnp.sum(upstream * unit_rows, axis=0), jnp.sum(upstream, axis=0))


def block_scores(query_rows, key_rows, seg_row, first_row):
    scale = 1.0 / math.sqrt(HD)
    scores = (
        jnp.einsum("qhd,khd->hqk", query_rows, key_rows, preferred_element_type=jnp.float32) * scale
    )
    query_pos = first_row + jnp.arange(query_rows.shape[0], dtype=jnp.int32)
    key_pos = jnp.arange(key_rows.shape[0], dtype=jnp.int32)
    seg_query = seg_row[first_row : first_row + query_rows.shape[0]]
    allowed = (seg_query[:, None] == seg_row[None, :]) & (key_pos[None, :] <= query_pos[:, None])
    return jnp.where(allowed[None], scores, masked_value)


def dispatch_table(routes, capacity, experts, slots):
    onehot = (routes[:, None] == jnp.arange(experts, dtype=jnp.int32)[None, :]).astype(jnp.int32)
    before = jnp.cumsum(onehot, axis=0) - onehot
    slot_rank = jnp.sum(before * onehot, axis=1)
    cap_limit = jnp.sum(capacity[None, :] * onehot, axis=1)
    target = jnp.where(slot_rank < cap_limit, routes * slots + slot_rank, -1)
    return (target[:, None] == jnp.arange(experts * slots, dtype=jnp.int32)[None, :]).astype(
        jnp.bfloat16
    )


def contract_rows(left, right):
    return lax.dot_general(
        left, right, (((0,), (0,)), ((), ())), preferred_element_type=jnp.float32
    )


def contract_cols(left, right):
    return lax.dot_general(
        left, right, (((1,), (1,)), ((), ())), preferred_element_type=jnp.float32
    )


def fanout(piece):
    return lax.all_gather(piece, "tp", axis=2, tiled=True)


def share_sum(terms):
    return lax.psum_scatter(
        terms.astype(jnp.bfloat16), "tp", scatter_dimension=2, tiled=True
    ).astype(jnp.float32)


def share_back(rows):
    return lax.all_to_all(rows, "ep", split_axis=0, concat_axis=0, tiled=True)


def local(
    tokens,
    segments,
    routes,
    capacity,
    ln1_gain,
    ln1_bias,
    qkv_weight,
    out_weight,
    ln2_gain,
    ln2_bias,
    mix_weight,
    up_weight,
    down_weight,
    expert_up,
    expert_down,
    cotangent,
):
    tok_rows, width = tokens.shape
    seq_count, seq_len = segments.shape
    local_width = out_weight.shape[0]
    local_heads = local_width // HD
    experts = capacity.shape[0]
    slots = 3 * tok_rows // (2 * experts)
    block_len = min(block_limit, seq_len)
    scale = 1.0 / math.sqrt(HD)
    col_share = width // lax.axis_size("tp")
    col_start = lax.axis_index("tp") * col_share
    input_values = tokens.astype(jnp.float32)
    first_norm, first_unit, first_spread = layer_norm(input_values, ln1_gain, ln1_bias)
    first_low = first_norm.astype(jnp.bfloat16)
    projected = jnp.einsum(
        "td,jdk->jtk", first_low, qkv_weight, preferred_element_type=jnp.float32
    ).astype(jnp.bfloat16)
    split_heads = projected.reshape(3, seq_count, seq_len, local_heads, HD)
    attended = []
    kept_sums = []
    sequence = 0
    for first_row in range(0, seq_len, block_len):
        query_rows = split_heads[0, sequence, first_row : first_row + block_len]
        scores = block_scores(query_rows, split_heads[1, sequence], segments[sequence], first_row)
        highest_score = jnp.max(scores, axis=-1, keepdims=True)
        exponent = jnp.exp(scores - highest_score)
        total_mass = jnp.sum(exponent, axis=-1, keepdims=True)
        chances = (exponent / total_mass).astype(jnp.bfloat16)
        kept_sums.append(highest_score + jnp.log(total_mass))
        attended.append(
            jnp.einsum(
                "hqk,khd->qhd",
                chances,
                split_heads[2, sequence],
                preferred_element_type=jnp.float32,
            )
        )
    heads_out = (
        jnp.concatenate(attended, axis=0).reshape(tok_rows, local_width).astype(jnp.bfloat16)
    )
    attn_part = jnp.dot(heads_out, out_weight, preferred_element_type=jnp.float32).astype(
        jnp.bfloat16
    )
    hidden = input_values + lax.psum(attn_part, "tp").astype(jnp.float32)
    second_norm, second_unit, second_spread = layer_norm(hidden, ln2_gain, ln2_bias)
    second_low = second_norm.astype(jnp.bfloat16)
    mixing = jax.nn.softmax(
        jnp.dot(second_low, mix_weight, preferred_element_type=jnp.float32), axis=-1
    )
    pre_dense = jnp.dot(second_low, up_weight, preferred_element_type=jnp.float32)
    act_dense = jax.nn.gelu(pre_dense).astype(jnp.bfloat16)
    dense_part = jnp.dot(act_dense, down_weight, preferred_element_type=jnp.float32)
    grad_out = cotangent.astype(jnp.float32)
    onehot_table = dispatch_table(routes, capacity, experts, slots)
    outgoing = (
        contract_rows(onehot_table, second_low).astype(jnp.bfloat16).reshape(experts, slots, width)
    )
    own_cols = lax.dynamic_slice_in_dim(outgoing, col_start, col_share, 2)
    received = fanout(lax.all_to_all(own_cols, "ep", split_axis=0, concat_axis=0, tiled=True))
    row_block = received.reshape(-1, width)
    pre_rows = jnp.dot(row_block, expert_up[0], preferred_element_type=jnp.float32)
    act_rows = jax.nn.gelu(pre_rows).astype(jnp.bfloat16)
    part_rows = jnp.dot(act_rows, expert_down[0], preferred_element_type=jnp.float32).astype(
        jnp.bfloat16
    )
    lead = received.shape[:2]
    part_rows, pre_rows, full_rows = (
        part_rows.reshape(lead + (width,)),
        pre_rows.reshape(lead + (pre_rows.shape[-1],)),
        received,
    )
    expert_share = share_sum(part_rows.astype(jnp.float32)).astype(jnp.bfloat16)
    returned = share_back(expert_share)
    expert_cols = jnp.dot(
        onehot_table,
        returned.reshape(experts * slots, col_share),
        preferred_element_type=jnp.float32,
    )
    dense_cols = share_sum(dense_part[None])[0]
    hidden_cols = lax.dynamic_slice_in_dim(hidden, col_start, col_share, 1)
    cot_cols = lax.dynamic_slice_in_dim(grad_out, col_start, col_share, 1)
    out_cols = hidden_cols + mixing[:, 0:1] * dense_cols + mixing[:, 1:2] * expert_cols
    mix_part = jnp.stack(
        [jnp.sum(cot_cols * dense_cols, axis=1), jnp.sum(cot_cols * expert_cols, axis=1)], axis=1
    )
    gathered_out, gathered_mix = (
        lax.all_gather(out_cols.astype(jnp.bfloat16), "tp", axis=1, tiled=True).astype(
            out_cols.dtype
        ),
        lax.all_gather(mix_part.astype(jnp.bfloat16), "tp", axis=1, tiled=True).astype(
            mix_part.dtype
        ),
    )
    grad_mixing = jnp.sum(gathered_mix.reshape(tok_rows, -1, 2), axis=1)
    grad_dense = (mixing[:, 0:1] * grad_out).astype(jnp.bfloat16)
    grad_down = contract_rows(act_dense, grad_dense)
    grad_act = contract_cols(grad_dense, down_weight)
    _, dense_gelu_back = jax.vjp(jax.nn.gelu, pre_dense)
    grad_pre = dense_gelu_back(grad_act)[0].astype(jnp.bfloat16)
    grad_up = contract_rows(second_low, grad_pre)
    grad_second = contract_cols(grad_pre, up_weight)
    grad_rows = (
        contract_rows(onehot_table, (mixing[:, 1:2] * grad_out).astype(jnp.bfloat16))
        .astype(jnp.bfloat16)
        .reshape(experts, slots, width)
    )
    grad_cols = lax.dynamic_slice_in_dim(grad_rows, col_start, col_share, 2)
    grad_in = fanout(lax.all_to_all(grad_cols, "ep", split_axis=0, concat_axis=0, tiled=True))
    rows_input = full_rows.reshape(-1, width)
    rows_grad = grad_in.reshape(-1, width)
    rows_pre = pre_rows.reshape(rows_input.shape[0], -1)
    rows_act, expert_gelu_back = jax.vjp(jax.nn.gelu, rows_pre)
    grad_expert_down = contract_rows(rows_act.astype(jnp.bfloat16), rows_grad)
    grad_rows_act = contract_cols(rows_grad, expert_down[0])
    grad_rows_pre = expert_gelu_back(grad_rows_act)[0].astype(jnp.bfloat16)
    grad_expert_up = contract_rows(rows_input, grad_rows_pre)
    grad_rows_in = (
        contract_cols(grad_rows_pre, expert_up[0]).astype(jnp.bfloat16).reshape(grad_in.shape)
    )
    grad_share = share_sum(grad_rows_in.astype(jnp.float32)).astype(jnp.bfloat16)
    grad_back = share_back(grad_share)
    expert_grad_cols = jnp.dot(
        onehot_table,
        grad_back.reshape(experts * slots, col_share),
        preferred_element_type=jnp.float32,
    )
    dense_grad_cols = share_sum(grad_second[None])[0]
    grad_second = lax.all_gather(
        (dense_grad_cols + expert_grad_cols).astype(jnp.bfloat16), "tp", axis=1, tiled=True
    ).astype(jnp.float32)
    grad_logits = mixing * (grad_mixing - jnp.sum(mixing * grad_mixing, axis=1, keepdims=True))
    mix_float = mix_weight.astype(jnp.float32)
    grad_second = grad_second + lax.dot_general(
        grad_logits, mix_float, (((1,), (1,)), ((), ())), precision=lax.Precision.HIGHEST
    )
    grad_mix_weight = lax.dot_general(
        second_low.astype(jnp.float32),
        grad_logits,
        (((0,), (0,)), ((), ())),
        precision=lax.Precision.HIGHEST,
    )
    grad_norm_two, grad_gain_two, grad_bias_two = norm_back(
        grad_second, second_unit, second_spread, ln2_gain
    )
    grad_hidden = grad_out + grad_norm_two
    grad_attn = grad_hidden.astype(jnp.bfloat16)
    grad_out_weight = contract_rows(heads_out, grad_attn)
    grad_heads = contract_cols(grad_attn, out_weight).astype(jnp.bfloat16)
    grad_split = grad_heads.reshape(seq_count, seq_len, local_heads, HD)
    query_grads = []
    position = 0
    sequence = 0
    key_rows = split_heads[1, sequence]
    value_rows = split_heads[2, sequence]
    key_total = jnp.zeros((seq_len, local_heads, HD), jnp.float32)
    value_total = jnp.zeros((seq_len, local_heads, HD), jnp.float32)
    for first_row in range(0, seq_len, block_len):
        query_rows = split_heads[0, sequence, first_row : first_row + block_len]
        scores = block_scores(query_rows, key_rows, segments[sequence], first_row)
        chances = jnp.exp(scores - kept_sums[position])
        position = position + 1
        upstream = grad_split[sequence, first_row : first_row + block_len]
        grad_chances = jnp.einsum(
            "qhd,khd->hqk", upstream, value_rows, preferred_element_type=jnp.float32
        )
        grad_scores = (
            chances * (grad_chances - jnp.sum(chances * grad_chances, axis=-1, keepdims=True))
        ).astype(jnp.bfloat16)
        value_total = value_total + jnp.einsum(
            "hqk,qhd->khd",
            chances.astype(jnp.bfloat16),
            upstream,
            preferred_element_type=jnp.float32,
        )
        query_grads.append(
            jnp.einsum("hqk,khd->qhd", grad_scores, key_rows, preferred_element_type=jnp.float32)
            * scale
        )
        key_total = (
            key_total
            + jnp.einsum(
                "hqk,qhd->khd", grad_scores, query_rows, preferred_element_type=jnp.float32
            )
            * scale
        )
    key_grads = [key_total]
    value_grads = [value_total]
    grad_query = jnp.concatenate(query_grads, axis=0).reshape(tok_rows, local_width)
    grad_key = jnp.stack(key_grads).reshape(tok_rows, local_width)
    grad_value = jnp.stack(value_grads).reshape(tok_rows, local_width)
    grad_projected = jnp.stack([grad_query, grad_key, grad_value]).astype(jnp.bfloat16)
    grad_qkv_weight = jnp.einsum(
        "td,jtk->jdk", first_low, grad_projected, preferred_element_type=jnp.float32
    )
    grad_first = jnp.einsum(
        "jtk,jdk->td", grad_projected, qkv_weight, preferred_element_type=jnp.float32
    )
    grad_first = lax.psum(grad_first.astype(jnp.bfloat16), "tp").astype(jnp.float32)
    grad_norm_one, grad_gain_one, grad_bias_one = norm_back(
        grad_first, first_unit, first_spread, ln1_gain
    )
    grad_tokens = (grad_hidden + grad_norm_one).astype(jnp.bfloat16)
    summed = (
        lax.psum(grad_qkv_weight.astype(jnp.bfloat16), "ep").astype(jnp.float32),
        lax.psum(grad_out_weight.astype(jnp.bfloat16), "ep").astype(jnp.float32),
        lax.psum(grad_up.astype(jnp.bfloat16), "ep").astype(jnp.float32),
        lax.psum(grad_down.astype(jnp.bfloat16), "ep").astype(jnp.float32),
        lax.psum(grad_mix_weight.astype(jnp.bfloat16), "ep").astype(jnp.float32),
        lax.psum(grad_gain_one.astype(jnp.bfloat16), "ep").astype(jnp.float32),
        lax.psum(grad_bias_one.astype(jnp.bfloat16), "ep").astype(jnp.float32),
        lax.psum(grad_gain_two.astype(jnp.bfloat16), "ep").astype(jnp.float32),
        lax.psum(grad_bias_two.astype(jnp.bfloat16), "ep").astype(jnp.float32),
    )
    return (
        gathered_out.astype(jnp.bfloat16),
        grad_tokens,
        summed[5],
        summed[6],
        summed[0],
        summed[1],
        summed[7],
        summed[8],
        summed[4],
        summed[2],
        summed[3],
        grad_expert_up[None],
        grad_expert_down[None],
    )


def solution(mesh):
    return jax.shard_map(
        local,
        mesh=mesh,
        in_specs=(
            P("ep", None),
            P("ep", None),
            P("ep"),
            P(),
            P(),
            P(),
            P(None, None, "tp"),
            P("tp", None),
            P(),
            P(),
            P(),
            P(None, "tp"),
            P("tp", None),
            P("ep", None, "tp"),
            P("ep", "tp", None),
            P("ep", None),
        ),
        out_specs=(
            P("ep", None),
            P("ep", None),
            P(),
            P(),
            P(None, None, "tp"),
            P("tp", None),
            P(),
            P(),
            P(),
            P(None, "tp"),
            P("tp", None),
            P("ep", None, "tp"),
            P("ep", "tp", None),
        ),
        check_vma=False,
    )
```

profile of v0, /device:TPU:0, one launch (start us, length us, event | category | flops | bytes accessed | tf_op | source)
XLA Modules:
  0.0 776.4 jit_solution(2730842598050736886)
XLA Ops:
  33.3 51.0 %all-reduce.6.cloned.1.call-done = bf16[1024,1024]{1,0:T(8,128)(2,1)} async-done(((bf16[1024,1024]{1,0:T(8,128)(2,1)}), bf16[1024,1024]{1,0:T(8,128)(2,1)}) %all-reduce.6.cloned.1.call-update) | async-done | bytes 2097168 | tf_op jit(solution)/shard_map/psum | solution.py:142
  84.3 3.0 fusion.103
  89.8 3.9 fusion.46
  93.8 25.5 %all_to_all.20 = bf16[8,192,256]{2,1,0:T(8,128)(2,1)} all-to-all(bf16[8,192,256]{2,1,0:T(8,128)(2,1)S(1)} %constant_dynamic-slice_fusion.1), channel_id=1, replica_groups=mesh['tp'=4,'ep'=8] {'ep'}, dimensions={0} | all-to-all | bytes 1572864 | tf_op jit(solution)/shard_map/all_to_all | solution.py:157
  119.3 27.3 %all-gather.6.cloned.1.call-done = bf16[8,192,1024]{2,1,0:T(8,128)(2,1)} async-done(((bf16[8,192,256]{2,1,0:T(8,128)(2,1)}), bf16[8,192,1024]{2,1,0:T(8,128)(2,1)}) %all-gather.6.cloned.1.call-update) | async-done | bytes 3145744 | tf_op jit(solution)/shard_map/all_gather | solution.py:69
  146.7 6.0 fusion.59
  152.7 5.3 convolution_convert_fusion.1
  158.6 4.7 fusion.111
  165.3 4.0 convert_bitcast_fusion.1
  169.3 26.9 %reduce-scatter.7.cloned.1.call-done = bf16[8,192,256]{2,1,0:T(8,128)(2,1)} async-done(((bf16[8,192,1024]{2,1,0:T(8,128)(2,1)}), bf16[8,192,256]{2,1,0:T(8,128)(2,1)}) %reduce-scatter.7.cloned.1.call-update) | async-done | bytes 786448 | tf_op jit(solution)/shard_map/reduce_scatter | solution.py:73
  196.2 5.5 all-to-all-start.1
  201.8 4.2 convert_element_type.212
  206.7 23.9 %reduce-scatter.5.cloned.1.call-done = bf16[1,1024,256]{2,1,0:T(8,128)(2,1)} async-done(((bf16[1,1024,1024]{2,1,0:T(8,128)(2,1)}), bf16[1,1024,256]{2,1,0:T(8,128)(2,1)}) %reduce-scatter.5.cloned.1.call-update) | async-done | bytes 524304 | tf_op jit(solution)/shard_map/reduce_scatter | solution.py:73
  230.7 3.9 fusion.86
  234.6 5.2 all-gather
  239.9 5.7 fusion.47
  245.7 26.0 %all_to_all.21 = bf16[8,192,256]{2,1,0:T(8,128)(2,1)} all-to-all(bf16[8,192,256]{2,1,0:T(8,128)(2,1)S(1)} %constant_dynamic-slice_fusion), channel_id=1, replica_groups=mesh['tp'=4,'ep'=8] {'ep'}, dimensions={0} | all-to-all | bytes 1572864 | tf_op jit(solution)/shard_map/all_to_all | solution.py:206
  272.0 27.0 %all-gather.10.cloned.1.call-done = bf16[8,192,1024]{2,1,0:T(8,128)(2,1)} async-done(((bf16[8,192,256]{2,1,0:T(8,128)(2,1)}), bf16[8,192,1024]{2,1,0:T(8,128)(2,1)}) %all-gather.10.cloned.1.call-update) | async-done | bytes 3145744 | tf_op jit(solution)/shard_map/all_gather | solution.py:69
  299.0 10.3 %fusion.10 = bf16[1536,1024]{1,0:T(8,128)(2,1)S(1)} fusion(f32[1536,1024]{1,0:T(8,128)} %copy-done.51, bf16[1536,1024]{1,0:T(8,128)(2,1)} %bitcast.207, bf16[1,1024,1024]{2,1,0:T(8,128)(2,1)S(1)} %copy-done), kind=kOutput, calls=%fused_computation.24 | convolution fusion | flops 3252682752 | bytes 14680064 | tf_op jit(solution)/shard_map/dot_general | solution.py:63
  309.3 4.9 convolution_convert_fusion
  314.3 7.3 fusion.37
  322.9 3.7 convert_bitcast_fusion
  326.6 25.7 %reduce-scatter.11.cloned.1.call-done = bf16[8,192,256]{2,1,0:T(8,128)(2,1)} async-done(((bf16[8,192,1024]{2,1,0:T(8,128)(2,1)}), bf16[8,192,256]{2,1,0:T(8,128)(2,1)}) %reduce-scatter.11.cloned.1.call-update) | async-done | bytes 786448 | tf_op jit(solution)/shard_map/reduce_scatter | solution.py:73
  352.3 5.5 all-to-all-start.3
  357.9 29.0 %reduce-scatter.9.cloned.1.call-done = bf16[1,1024,256]{2,1,0:T(8,128)(2,1)} async-done(((bf16[1,1024,1024]{2,1,0:T(8,128)(2,1)}), bf16[1,1024,256]{2,1,0:T(8,128)(2,1)}) %reduce-scatter.9.cloned.1.call-update) | async-done | bytes 524304 | tf_op jit(solution)/shard_map/reduce_scatter | solution.py:73
  387.8 3.5 fusion.70
  391.8 22.5 %all-gather.12.cloned.1.call-done = bf16[1024,1024]{1,0:T(8,128)(2,1)} async-done(((bf16[1024,256]{1,0:T(8,128)(2,1)}), bf16[1024,1024]{1,0:T(8,128)(2,1)}) %all-gather.12.cloned.1.call-update) | async-done | bytes 2097168 | tf_op jit(solution)/shard_map/all_gather | solution.py:226
  414.3 6.3 multiply_reduce_fusion.2
  420.6 3.2 multiply_add_fusion
  428.8 4.3 multiply_reduce_fusion
  433.1 2.6 multiply_reduce_fusion.1
  438.9 2.8 fusion.92
  444.4 6.7 multiply_convert_fusion
  456.5 5.1 bitcast_convert_fusion
  461.7 2.5 fusion.85
  464.5 6.1 convolution_convert_fusion.3
  470.6 4.4 convolution_convert_fusion.2
  476.6 3.4 fusion.64
  480.0 2.5 convolution_convert_fusion.9
  482.6 8.5 %convolution_bitcast_fusion.1 = f32[1,1024,1024]{2,1,0:T(8,128)} fusion(bf16[1536,1024]{1,0:T(8,128)(2,1)} %bitcast.206, bf16[1536,1024]{1,0:T(8,128)(2,1)} %copy-done.50), kind=kOutput, calls=%fused_computation.88 | convolution fusion | flops 3221225472 | bytes 10485760 | tf_op jit(solution)/shard_map/dot_general | solution.py:57
  491.1 9.3 %convolution_bitcast_fusion = f32[1,1024,1024]{2,1,0:T(8,128)} fusion(bf16[1536,1024]{1,0:T(8,128)(2,1)S(1)} %bitcast.208, f32[1536,1024]{1,0:T(8,128)} %copy-done.51), kind=kOutput, calls=%fused_computation.87 | convolution fusion | flops 3235381248 | bytes 13631488 | tf_op jit(solution)/shard_map/dot_general | solution.py:57
  500.4 12.8 %all-reduce.8.cloned.1.call-done = bf16[1024,1024]{1,0:T(8,128)(2,1)} async-done(((bf16[1024,1024]{1,0:T(8,128)(2,1)}), bf16[1024,1024]{1,0:T(8,128)(2,1)}) %all-reduce.8.cloned.1.call-update) | async-done | bytes 2097168 | tf_op jit(solution)/shard_map/psum | solution.py:296
  515.2 3.5 fusion.30
  518.6 37.5 %all-reduce = (bf16[1024]{0:T(1024)(128)(2,1)S(1)}, bf16[1024]{0:T(1024)(128)(2,1)S(1)}, bf16[1024]{0:T(1024)(128)(2,1)S(1)}, bf16[1024]{0:T(1024)(128)(2,1)S(1)}, bf16[1024,2]{0,1:T(2,128)(2,1)S(1)}) all-reduce(bf16[1024]{0:T(1024)(128)(2,1)S(1)} %get-tuple-element.54, ...), channel_id=1, replica_groups=mesh['tp'=4,'ep'=8] {'ep'}, use_global_device_ids=true, to_apply=%region_31.32 | all-reduce | flops 6144 | bytes 24576 | tf_op jit(solution)/shard_map/psum | solution.py:307
  559.2 4.6 fusion.27
  563.8 193.9 %all-reduce.10.cloned.1.call-done = (bf16[3,1024,256]{1,2,0:T(8,128)(2,1)}, bf16[256,1024]{1,0:T(8,128)(2,1)}, bf16[1024,1024]{1,0:T(8,128)(2,1)}, bf16[1024,1024]{1,0:T(8,128)(2,1)}) async-done(((bf16[3,1024,256]{1,2,0:T(8,128)(2,1)}, bf16[256,1024]{1,0:T(8,128)(2,1)}, bf16[1024,1024]{1,0:T(8,128)(2,1)}, bf16[1024,1024]{1,0:T(8,128)(2,1)}), (bf16[3,1024,256]{1,2,0:T(8,128)(2,1)}, ...) | async-done | bytes 6291472 | tf_op jit(solution)/shard_map/psum | solution.py:302
  759.9 3.1 copy.58
  765.5 2.6 convert_element_type.249
  (211 shorter events, 64.1 us)
Async XLA Ops:
  7.2 145.5 %copy-start = (bf16[1,1024,1024]{2,1,0:T(8,128)(2,1)S(1)}, bf16[1,1024,1024]{2,1,0:T(8,128)(2,1)}, u32[]{:S(2)}) copy-start(bf16[1,1024,1024]{2,1,0:T(8,128)(2,1)} %param.30) | copy-start | bytes 6291460
  7.2 4.6 copy-start.39
  7.2 4.6 copy-start.37
  7.2 4.6 copy-start.48
  7.2 77.1 %all-reduce.6.cloned.1.call-start = ((), (), s32[]{:S(2)}) async-start(), calls=%async_computation.8 | async-start | bytes 4194304 | tf_op jit(solution)/shard_map/psum | solution.py:142
  7.3 4.6 copy-start.4
  7.3 4.6 copy-start.47
  9.4 4.6 copy-start.31
  19.0 5.9 copy-start.3
  27.1 6.1 copy-start.42
  30.1 116.6 %all-gather.6.cloned.1.call-start = ((), (), s32[]{:S(2)}) async-start(), calls=%async_computation.10 | async-start | bytes 3932160 | tf_op jit(solution)/shard_map/all_gather | solution.py:69
  33.3 55.4 %copy-start.36 = (f32[1024]{0:T(1024)S(1)}, f32[1024]{0:T(1024)}, u32[]{:S(2)}) copy-start(f32[1024]{0:T(1024)} %param.24) | copy-start | bytes 12292
  33.3 55.4 %copy-start.40 = (f32[1024]{0:T(1024)S(1)}, f32[1024]{0:T(1024)}, u32[]{:S(2)}) copy-start(f32[1024]{0:T(1024)} %param.25) | copy-start | bytes 12292
  119.3 76.9 %reduce-scatter.7.cloned.1.call-start = ((), (), s32[]{:S(2)}) async-start(), calls=%async_computation.11 | async-start | bytes 3932160 | tf_op jit(solution)/shard_map/reduce_scatter | solution.py:73
  152.7 5.4 copy-start.51
  158.1 72.5 %reduce-scatter.5.cloned.1.call-start = ((), (), s32[]{:S(2)}) async-start(), calls=%async_computation.9 | async-start | bytes 2621440 | tf_op jit(solution)/shard_map/reduce_scatter | solution.py:73
  158.6 6.7 copy-start.45
  169.3 36.7 %copy-start.41 = (bf16[1024,2]{0,1:T(2,128)(2,1)S(1)}, bf16[1024,2]{0,1:T(2,128)(2,1)}, u32[]{:S(2)}) copy-start(bf16[1024,2]{0,1:T(2,128)(2,1)} %param.26) | copy-start | bytes 12292
  196.2 34.4 %all-to-all-start.1 = ((bf16[8,192,256]{2,1,0:T(8,128)(2,1)}), bf16[8,192,256]{2,1,0:T(8,128)(2,1)}, u32[]{:S(2)}, u32[]{:S(2)}) async-start(bf16[8,192,256]{2,1,0:T(8,128)(2,1)} %reduce-scatter.7.cloned.1.call-done), calls=%async_computation.3 | async-start | bytes 1572864 | tf_op jit(solution)/shard_map/all_to_all | solution.py:79
  201.7 97.2 %all-gather.10.cloned.1.call-start = ((), (), s32[]{:S(2)}) async-start(), calls=%async_computation.14 | async-start | bytes 3932160 | tf_op jit(solution)/shard_map/all_gather | solution.py:69
  201.8 4.2 copy-start.12
  271.8 80.6 %reduce-scatter.11.cloned.1.call-start = ((), (), s32[]{:S(2)}) async-start(), calls=%async_computation.15 | async-start | bytes 3932160 | tf_op jit(solution)/shard_map/reduce_scatter | solution.py:73
  299.0 10.3 %copy-start.44 = (bf16[1,1024,1024]{2,1,0:T(8,128)(2,1)S(1)}, bf16[1,1024,1024]{2,1,0:T(8,128)(2,1)}, u32[]{:S(2)}) copy-start(bf16[1,1024,1024]{2,1,0:T(8,128)(2,1)} %param.29) | copy-start | bytes 6291460
  309.2 5.0 copy-start.50
  309.3 5.0 copy-start.16
  314.2 72.7 %reduce-scatter.9.cloned.1.call-start = ((), (), s32[]{:S(2)}) async-start(), calls=%async_computation.13 | async-start | bytes 2621440 | tf_op jit(solution)/shard_map/reduce_scatter | solution.py:73
  314.3 8.6 %copy-start.46 = (bf16[1024,1024]{1,0:T(8,128)(2,1)S(1)}, bf16[1024,1024]{1,0:T(8,128)(2,1)}, u32[]{:S(2)}) copy-start(bf16[1024,1024]{1,0:T(8,128)(2,1)} %param.27) | copy-start | bytes 6291460
  352.3 34.6 %all-to-all-start.3 = ((bf16[8,192,256]{2,1,0:T(8,128)(2,1)}), bf16[8,192,256]{2,1,0:T(8,128)(2,1)S(1)}, u32[]{:S(2)}, u32[]{:S(2)}) async-start(bf16[8,192,256]{2,1,0:T(8,128)(2,1)} %reduce-scatter.11.cloned.1.call-done), calls=%async_computation.7 | async-start | bytes 1572864 | tf_op jit(solution)/shard_map/all_to_all | solution.py:79
  357.9 56.4 %all-gather.12.cloned.1.call-start = ((), (), s32[]{:S(2)}) async-start(), calls=%async_computation.16 | async-start | bytes 2621440 | tf_op jit(solution)/shard_map/all_gather | solution.py:226
  387.8 26.5 %copy-start.6 = (bf16[1024,1024]{1,0:T(8,128)(2,1)S(1)}, bf16[1024,1024]{1,0:T(8,128)(2,1)}, u32[]{:S(2)}) copy-start(bf16[1024,1024]{1,0:T(8,128)(2,1)} %param.16) | copy-start | bytes 6291460
  391.3 121.9 %all-reduce.8.cloned.1.call-start = ((), (), s32[]{:S(2)}) async-start(), calls=%async_computation.17 | async-start | bytes 4194304 | tf_op jit(solution)/shard_map/psum | solution.py:296
  414.3 6.3 copy-start.10
  414.3 6.3 copy-start.17
  420.6 4.0 slice-start
  420.6 6.5 slice-start.1
  423.8 5.0 copy-start.7
  427.1 6.0 slice-start.2
  428.8 4.3 slice-start.3
  456.5 5.2 copy-start.26
  461.7 102.1 %all-gather.8.cloned.1.call-start = ((), (), s32[]{:S(2)}) async-start(), calls=%async_computation.12 | async-start | bytes 2621440 | tf_op jit(solution)/shard_map/all_gather | solution.py:185
  464.3 293.4 %all-reduce.10.cloned.1.call-start = ((), (), s32[]{:S(2)}) async-start(), calls=%async_computation.18 | async-start | bytes 12582912 | tf_op jit(solution)/shard_map/psum | solution.py:302
  464.5 6.1 copy-start.18
  464.5 6.1 copy-start.53
  470.6 4.4 copy-start.8
  470.6 4.4 copy-start.20
  482.6 8.6 %copy-start.43 = (bf16[8,192,1024]{2,1,0:T(8,128)(2,1)S(1)}, bf16[8,192,1024]{2,1,0:T(8,128)(2,1)}, u32[]{:S(2)}) copy-start(bf16[8,192,1024]{2,1,0:T(8,128)(2,1)} %all-gather.10.cloned.1.call-done) | copy-start | bytes 9437188
  757.7 5.3 copy-start.23
  765.5 4.1 copy-start.1
  (24 other events, 53.1 us)
Sparse Core Ops, SparseCore 0:
  30.2 54.0 all-reduce.5
  119.4 27.2 all-gather.5
  158.2 37.9 reduce-scatter.6
  199.2 31.4 reduce-scatter.4
  271.9 27.0 all-gather.9
  314.4 37.9 reduce-scatter.10
  355.4 31.4 reduce-scatter.8
  391.4 22.8 all-gather.11
  461.8 51.3 all-reduce.7
  515.2 22.9 all-gather.7
  543.2 214.4 all-reduce.9
where the time goes:
time: 785 us; the launch traced here: 776 us
  waiting for transfers between devices  440 us (56%)
  matrix products  142 us (18%)
  blocking collectives  94.2 us (12%)
  other arithmetic  55.9 us (7%)
  local copies, waits for them, and re-layouts  16.4 us (2%)
  between operations  15 us (2%)
  starting transfers between devices  12.9 us (2%)
    psum x1, waiting for transfers between devices, local(): lax.psum(grad_qkv_weight.astype(jnp.bfloat16), 'ep').astype(jnp.float32)  194 us
    reduce_scatter x4, waiting for transfers between devices, share_sum(): lax.psum_scatter(terms.astype(jnp.bfloat16), 'tp', scatter_dimension=2, t...  106 us
    all_gather x2, waiting for transfers between devices, fanout(): return lax.all_gather(piece, 'tp', axis=2, tiled=True)  54.3 us
    psum x1, waiting for transfers between devices, local(): hidden = input_values + lax.psum(attn_part, 'tp').astype(jnp.float32)  51 us
    dot_general x7, matrix products, contract_rows(): lax.dot_general(left, right, (((0,), (0,)), ((), ())), preferred_element_...  39.4 us
    psum x1, blocking collectives, local(): lax.psum(grad_gain_one.astype(jnp.bfloat16), 'ep').astype(jnp.float32)  37.5 us
    dot_general x5, matrix products, contract_cols(): lax.dot_general(left, right, (((1,), (1,)), ((), ())), preferred_element_...  27 us
    all_to_all x1, blocking collectives, local(): lax.all_to_all(grad_cols, 'ep', split_axis=0, concat_axis=0, tiled=True)  26 us
  transfers between devices with their start and end apart: 13, of which 10 were waited for; matrix products, arithmetic and copies ran while one was open for 10% of the time, Pallas kernels for 0%

commit v1 on v0

--- a/solution.py
+++ b/solution.py
@@ -1,15 +1,306 @@
+import functools
 import math
 
 import jax
 import jax.numpy as jnp
 from jax import lax
+from jax.experimental import pallas as pl
+from jax.experimental.pallas import tpu as pltpu
 from jax.sharding import PartitionSpec as P
 
 HD = 64
-
-
 epsilon = 1e-05
 masked_value = -1e30
+F32 = jnp.float32
+BF16 = jnp.bfloat16
+VMEM_LIMIT = 60 * 2**20
+MESH = pl.DeviceIdType.MESH
+
+
+def mm(a, b):
+    return lax.dot_general(a, b, (((1,), (0,)), ((), ())), preferred_element_type=F32)
+
+
+def mm_t(a, b):
+    return lax.dot_general(a, b, (((1,), (1,)), ((), ())), preferred_element_type=F32)
+
+
+def t_mm(a, b):
+    return lax.dot_general(a, b, (((0,), (0,)), ((), ())), preferred_element_type=F32)
+
+
+def norm_rows(x):
+    centred = x - jnp.mean(x, axis=-1, keepdims=True)
+    spread = lax.rsqrt(jnp.mean(centred * centred, axis=-1, keepdims=True) + epsilon)
+    return centred * spread, spread
+
+
+def place():
+    t = lax.axis_index("tp")
+    return t, lax.div(t, 2), lax.rem(t, 2), lax.axis_index("ep")
+
+
+def remote(src, dst, send, recv, t, e):
+    return pltpu.make_async_remote_copy(
+        src_ref=src, dst_ref=dst, send_sem=send, recv_sem=recv, device_id=(t, e), device_id_type=MESH
+    )
+
+
+def greet(partners, loop_partner, loop_count):
+    bar = pltpu.get_barrier_semaphore()
+    for t, e in partners:
+        pl.semaphore_signal(bar, inc=1, device_id=(t, e), device_id_type=MESH)
+
+    def one(i, carry):
+        t, e = loop_partner(i)
+        pl.semaphore_signal(bar, inc=1, device_id=(t, e), device_id_type=MESH)
+        return carry
+
+    if loop_count:
+        lax.fori_loop(0, loop_count, one, 0)
+    pl.semaphore_wait(bar, len(partners) + loop_count)
+
+
+def onehot_rows(tgt, first, count):
+    rows = lax.broadcasted_iota(jnp.int32, (count, tgt.shape[1]), 0) + first
+    return (rows == tgt).astype(F32).astype(BF16)
+
+
+def forward_kernel(
+    n_tp, n_ep, tok, cot, segr, segc, rts, cap, g1, b1, g2, b2, wqkv, wout, mixw,
+    qkv_o, ht_o, lse_o, n2_o, attn_o, mix_o, crow_o, tgt_o,
+    n1, vt, snd, part, cbuf, xbuf, bias,
+    as_, ar_, fs_, fr_, cs_, cr_, xs_, xr_, gs_, gr_, lsem,
+):
+    t, x, c, e = place()
+    nx = n_tp // 2
+    rows_all, width = tok.shape
+    half = width // 2
+    experts, slots = snd.shape[0], snd.shape[1]
+    wl = wout.shape[0]
+    heads = wl // HD
+    blk = rows_all // 4
+    mate = 2 * x + 1 - c
+    x_peers = [2 * lax.rem(x + d, nx) + c for d in range(1, nx)]
+    greet([(mate, e)] + [(p, e) for p in x_peers], lambda i: (t, lax.rem(e + 1 + i, n_ep)), n_ep - 1)
+
+    hot = lax.broadcasted_iota(jnp.int32, (experts, rows_all), 0) == rts[...]
+    hot_f = hot.astype(F32)
+    hot_b = hot_f.astype(BF16)
+    counts = jnp.zeros((experts, rows_all), F32)
+    for k in range(4):
+        earlier = (
+            lax.broadcasted_iota(jnp.int32, (blk, rows_all), 0) + k * blk
+            < lax.broadcasted_iota(jnp.int32, (blk, rows_all), 1)
+        )
+        counts = counts + mm(hot_b[:, k * blk : (k + 1) * blk], earlier.astype(F32).astype(BF16))
+    rank = jnp.sum(counts * hot_f, axis=0, keepdims=True).astype(jnp.int32)
+    limit = jnp.sum(jnp.where(hot, cap[...], 0), axis=0, keepdims=True)
+    tgt = jnp.where(rank < limit, rts[...] * slots + rank, -1)
+    tgt_o[...] = tgt
+
+    my_half = pl.ds(pl.multiple_of(c * half, half), half)
+
+    def rows_for(dest):
+        hot_rows = onehot_rows(tgt_o[...], dest * slots, slots)
+        return mm(hot_rows, cot[:, my_half]).astype(BF16)
+
+    def a2a_copy(dest, src):
+        return remote(snd.at[dest], crow_o.at[c, src], as_.at[dest], ar_.at[src], t, dest)
+
+    def send_rows(i, carry):
+        dest = lax.rem(e + 1 + i, n_ep)
+        snd[dest] = rows_for(dest)
+        a2a_copy(dest, e).start()
+        return carry
+
+    lax.fori_loop(0, n_ep - 1, send_rows, 0)
+    snd[e] = rows_for(e)
+    own = pltpu.make_async_copy(snd.at[e], crow_o.at[c, e], lsem)
+    own.start()
+    remote(snd.at[e], crow_o.at[c, e], fs_.at[e], fr_.at[e], mate, e).start()
+
+    for i in range(4):
+        rs = pl.ds(i * blk, blk)
+        unit, _ = norm_rows(tok[rs, :].astype(F32))
+        normed = (unit * g1[...] + b1[...]).astype(BF16)
+        n1[rs, :] = normed
+        for j in range(3):
+            qkv_o[j, rs, :] = mm(normed, wqkv[j]).astype(BF16)
+        vt[:, rs] = qkv_o[2, rs, :].astype(F32).T.astype(BF16)
+
+    def chunk(i):
+        return pl.ds(i * blk, blk)
+
+    other_half = pl.ds(pl.multiple_of((1 - c) * half, half), half)
+
+    def core_copy(i):
+        return remote(part.at[chunk(i), other_half], cbuf.at[chunk(i)], cs_.at[i], cr_.at[i], mate, e)
+
+    def x_copy(i, d):
+        return remote(
+            xbuf.at[x, chunk(i)], xbuf.at[x, chunk(i)], xs_.at[i, d - 1], xr_.at[i, d - 1], x_peers[d - 1], e
+        )
+
+    def x_arrival(i, d):
+        src = lax.rem(x + nx - d, nx)
+        return remote(
+            xbuf.at[src, chunk(i)], xbuf.at[src, chunk(i)], xs_.at[i, d - 1], xr_.at[i, d - 1], x_peers[d - 1], e
+        )
+
+    def share_copy(i):
+        return remote(
+            attn_o.at[chunk(i), my_half], attn_o.at[chunk(i), my_half], gs_.at[i], gr_.at[i], mate, e
+        )
+
+    def share_arrival(i):
+        return remote(
+            attn_o.at[chunk(i), other_half], attn_o.at[chunk(i), other_half], gs_.at[i], gr_.at[i], mate, e
+        )
+
+    def attend(i):
+        keys = (i + 1) * blk
+        ks = pl.ds(0, keys)
+        allowed = (segc[ks, :] == segr[:, chunk(i)]) & (
+            lax.broadcasted_iota(jnp.int32, (keys, blk), 0)
+            <= lax.broadcasted_iota(jnp.int32, (keys, blk), 1) + i * blk
+        )
+        bias[ks, :] = jnp.where(allowed, 0.0, masked_value)
+        head_of = lax.div(lax.broadcasted_iota(jnp.int32, (blk, wl), 1), HD)
+
+        def one_head(h, carry):
+            q_h = jnp.where(head_of == h, qkv_o[0, chunk(i), :].astype(F32) * 0.125, 0.0).astype(BF16)
+            scores = mm_t(qkv_o[1, ks, :], q_h) + bias[ks, :]
+            top = jnp.max(scores, axis=0, keepdims=True)
+            weights = jnp.exp(scores - top)
+            mass = jnp.sum(weights, axis=0, keepdims=True)
+            lse_o[pl.ds(h, 1), chunk(i)] = top + jnp.log(mass)
+            probs = (weights * (1.0 / mass)).astype(BF16)
+            hs = pl.ds(pl.multiple_of(h * HD, HD), HD)
+            ht_o[hs, chunk(i)] = mm(vt[hs, ks], probs).astype(BF16)
+            return carry
+
+        lax.fori_loop(0, heads, one_head, 0)
+        part[chunk(i), :] = t_mm(ht_o[:, chunk(i)], wout[...]).astype(BF16)
+        core_copy(i).start()
+
+    def sum_cores(i):
+        core_copy(i).wait_recv()
+        both = part[chunk(i), my_half].astype(F32) + cbuf[chunk(i), :].astype(F32)
+        xbuf[x, chunk(i), :] = both.astype(BF16)
+        for d in range(1, nx):
+            x_copy(i, d).start()
+
+    def sum_chips(i):
+        for d in range(1, nx):
+            x_arrival(i, d).wait_recv()
+        total = xbuf[0, chunk(i), :].astype(F32)
+        for j in range(1, nx):
+            total = total + xbuf[j, chunk(i), :].astype(F32)
+        attn_o[chunk(i), my_half] = total.astype(BF16)
+        share_copy(i).start()
+
+    def finish(i):
+        share_arrival(i).wait_recv()
+        hidden = tok[chunk(i), :].astype(F32) + attn_o[chunk(i), :].astype(F32)
+        unit, _ = norm_rows(hidden)
+        normed = (unit * g2[...] + b2[...]).astype(BF16)
+        n2_o[chunk(i), :] = normed
+        logits = mm(normed, mixw[...])
+        lane = lax.broadcasted_iota(jnp.int32, logits.shape, 1)
+        logits = jnp.where(lane < 2, logits, masked_value)
+        mix = jnp.exp(logits - jnp.max(logits, axis=1, keepdims=True))
+        mix_o[chunk(i), :] = mix / jnp.sum(mix, axis=1, keepdims=True)
+
+    attend(0)
+    attend(1)
+    sum_cores(0)
+    attend(2)
+    sum_cores(1)
+    attend(3)
+    sum_cores(2)
+    sum_cores(3)
+
+    def forward_rows(i, carry):
+        src = lax.rem(e + n_ep - 1 - i, n_ep)
+        a2a_copy(e, src).wait_recv()
+        remote(crow_o.at[c, src], crow_o.at[c, src], fs_.at[src], fr_.at[src], mate, e).start()
+        return carry
+
+    def forward_done(src, carry):
+        remote(crow_o.at[1 - c, src], crow_o.at[1 - c, src], fs_.at[src], fr_.at[src], mate, e).wait()
+        return carry
+
+    for i in range(4):
+        sum_chips(i)
+        if i >= 1:
+            finish(i - 1)
+    finish(3)
+    lax.fori_loop(0, n_ep - 1, forward_rows, 0)
+    lax.fori_loop(0, n_ep, forward_done, 0)
+    own.wait()
+
+    def sent(i, carry):
+        a2a_copy(lax.rem(e + 1 + i, n_ep), e).wait_send()
+        return carry
+
+    lax.fori_loop(0, n_ep - 1, sent, 0)
+    for i in range(4):
+        core_copy(i).wait_send()
+        for d in range(1, nx):
+            x_copy(i, d).wait_send()
+        share_copy(i).wait_send()
+
+
+def forward(tokens, cotangent, segments, routes, capacity, g1, b1, g2, b2, wqkv, wout, mix_weight):
+    n_tp, n_ep = lax.axis_size("tp"), lax.axis_size("ep")
+    rows, width = tokens.shape
+    wl = wout.shape[0]
+    experts = capacity.shape[0]
+    slots = 3 * rows // (2 * experts)
+    nx = n_tp // 2
+    half = width // 2
+    vm = pl.BlockSpec(memory_space=pltpu.VMEM)
+    dma = pltpu.SemaphoreType.DMA
+    shape = jax.ShapeDtypeStruct
+    mixw = jnp.pad(mix_weight, ((0, 0), (0, 126)))
+    return pl.pallas_call(
+        functools.partial(forward_kernel, n_tp, n_ep),
+        out_shape=(
+            shape((3, rows, wl), BF16),
+            shape((wl, rows), BF16),
+            shape((wl // HD, rows), F32),
+            shape((rows, width), BF16),
+            shape((rows, width), BF16),
+            shape((rows, 128), F32),
+            shape((2, experts, slots, half), BF16),
+            shape((1, rows), jnp.int32),
+        ),
+        in_specs=[vm] * 13,
+        out_specs=(vm,) * 6 + (pl.BlockSpec(memory_space=pl.ANY), vm),
+        scratch_shapes=[
+            pltpu.VMEM((rows, width), BF16),
+            pltpu.VMEM((wl, rows), BF16),
+            pltpu.VMEM((experts, slots, half), BF16),
+            pltpu.VMEM((rows, width), BF16),
+            pltpu.VMEM((rows, half), BF16),
+            pltpu.VMEM((nx, rows, half), BF16),
+            pltpu.VMEM((rows, rows // 4), F32),
+            dma((experts,)), dma((experts,)), dma((experts,)), dma((experts,)),
+            dma((4,)), dma((4,)), dma((4, max(nx - 1, 1))), dma((4, max(nx - 1, 1))), dma((4,)), dma((4,)),
+            dma,
+        ],
+        compiler_params=pltpu.CompilerParams(
+            collective_id=0, has_side_effects=True, vmem_limit_bytes=VMEM_LIMIT
+        ),
+        cost_estimate=pl.CostEstimate(flops=8 * 10**9, bytes_accessed=30 * 10**6, transcendentals=0),
+        name="attention_forward",
+    )(
+        tokens, cotangent, segments, segments.reshape(rows, 1), routes.reshape(1, rows),
+        capacity.reshape(experts, 1), g1.reshape(1, width), b1.reshape(1, width), g2.reshape(1, width),
+        b2.reshape(1, width), wqkv, wout, mixw,
+    )
+
 block_limit = 512
 
 
@@ -107,49 +398,26 @@
     scale = 1.0 / math.sqrt(HD)
     col_share = width // lax.axis_size("tp")
     col_start = lax.axis_index("tp") * col_share
+    (projected, heads_t, lse, second_low, attn_sum, mix_wide, cot_rows, targets) = forward(
+        tokens, cotangent, segments, routes, capacity, ln1_gain, ln1_bias, ln2_gain, ln2_bias,
+        qkv_weight, out_weight, mix_weight,
+    )
     input_values = tokens.astype(jnp.float32)
     first_norm, first_unit, first_spread = layer_norm(input_values, ln1_gain, ln1_bias)
     first_low = first_norm.astype(jnp.bfloat16)
-    projected = jnp.einsum(
-        "td,jdk->jtk", first_low, qkv_weight, preferred_element_type=jnp.float32
-    ).astype(jnp.bfloat16)
     split_heads = projected.reshape(3, seq_count, seq_len, local_heads, HD)
-    attended = []
-    kept_sums = []
-    sequence = 0
-    for first_row in range(0, seq_len, block_len):
-        query_rows = split_heads[0, sequence, first_row : first_row + block_len]
-        scores = block_scores(query_rows, split_heads[1, sequence], segments[sequence], first_row)
-        highest_score = jnp.max(scores, axis=-1, keepdims=True)
-        exponent = jnp.exp(scores - highest_score)
-        total_mass = jnp.sum(exponent, axis=-1, keepdims=True)
-        chances = (exponent / total_mass).astype(jnp.bfloat16)
-        kept_sums.append(highest_score + jnp.log(total_mass))
-        attended.append(
-            jnp.einsum(
-                "hqk,khd->qhd",
-                chances,
-                split_heads[2, sequence],
-                preferred_element_type=jnp.float32,
-            )
-        )
-    heads_out = (
-        jnp.concatenate(attended, axis=0).reshape(tok_rows, local_width).astype(jnp.bfloat16)
-    )
-    attn_part = jnp.dot(heads_out, out_weight, preferred_element_type=jnp.float32).astype(
-        jnp.bfloat16
-    )
-    hidden = input_values + lax.psum(attn_part, "tp").astype(jnp.float32)
-    second_norm, second_unit, second_spread = layer_norm(hidden, ln2_gain, ln2_bias)
-    second_low = second_norm.astype(jnp.bfloat16)
-    mixing = jax.nn.softmax(
-        jnp.dot(second_low, mix_weight, preferred_element_type=jnp.float32), axis=-1
-    )
+    kept_sums = [lse[:, i : i + block_len, None] for i in range(0, seq_len, block_len)]
+    heads_out = heads_t.T
+    hidden = input_values + attn_sum.astype(jnp.float32)
+    _, second_unit, second_spread = layer_norm(hidden, ln2_gain, ln2_bias)
+    mixing = mix_wide[:, :2]
     pre_dense = jnp.dot(second_low, up_weight, preferred_element_type=jnp.float32)
     act_dense = jax.nn.gelu(pre_dense).astype(jnp.bfloat16)
     dense_part = jnp.dot(act_dense, down_weight, preferred_element_type=jnp.float32)
     grad_out = cotangent.astype(jnp.float32)
-    onehot_table = dispatch_table(routes, capacity, experts, slots)
+    onehot_table = (
+        targets.reshape(-1, 1) == jnp.arange(experts * slots, dtype=jnp.int32)[None, :]
+    ).astype(jnp.bfloat16)
     outgoing = (
         contract_rows(onehot_table, second_low).astype(jnp.bfloat16).reshape(experts, slots, width)
     )
@@ -197,13 +465,11 @@
     grad_pre = dense_gelu_back(grad_act)[0].astype(jnp.bfloat16)
     grad_up = contract_rows(second_low, grad_pre)
     grad_second = contract_cols(grad_pre, up_weight)
-    grad_rows = (
-        contract_rows(onehot_table, (mixing[:, 1:2] * grad_out).astype(jnp.bfloat16))
-        .astype(jnp.bfloat16)
-        .reshape(experts, slots, width)
-    )
-    grad_cols = lax.dynamic_slice_in_dim(grad_rows, col_start, col_share, 2)
-    grad_in = fanout(lax.all_to_all(grad_cols, "ep", split_axis=0, concat_axis=0, tiled=True))
+    cot_all = jnp.concatenate([cot_rows[0], cot_rows[1]], axis=-1).reshape(-1, width)
+    mix_rows = jax.nn.softmax(
+        jnp.dot(row_block, mix_weight, preferred_element_type=jnp.float32), axis=-1
+    )
+    grad_in = (mix_rows[:, 1:2] * cot_all.astype(jnp.float32)).astype(jnp.bfloat16).reshape(received.shape)
     rows_input = full_rows.reshape(-1, width)
     rows_grad = grad_in.reshape(-1, width)
     rows_pre = pre_rows.reshape(rows_input.shape[0], -1)

time: 785 us -> 700 us (0.89)
  waiting for transfers between devices: 440 us -> 318 us
  Pallas kernels: 0 us -> 53.5 us
  blocking collectives: 94.2 us -> 66.7 us
  local copies, waits for them, and re-layouts: 16.4 us -> 29.9 us
    pallas_call x0 -> x1, Pallas kernels: none -> 53.5 us  [forward(): pl.pallas_call(functools.partial(forward_kernel, n_tp, n_ep), out_shape=(...]
    psum x1 -> x0, waiting for transfers between devices: 51 us -> none  [local(): hidden = input_values + lax.psum(attn_part, 'tp').astype(jnp.float32)]
    reduce_scatter x4, waiting for transfers between devices: 106 us -> 73.8 us  [share_sum(): lax.psum_scatter(terms.astype(jnp.bfloat16), 'tp', scatter_dimension=2, t...]
    all_gather x2 -> x1, waiting for transfers between devices: 54.3 us -> 23.2 us  [fanout(): return lax.all_gather(piece, 'tp', axis=2, tiled=True)]
    all_to_all x1 -> x0, blocking collectives: 26 us -> none  [local(): lax.all_to_all(grad_cols, 'ep', split_axis=0, concat_axis=0, tiled=True)]
    all_gather x1, waiting for transfers between devices: 22.5 us -> 12.3 us  [local(): lax.all_gather((dense_grad_cols + expert_grad_cols).astype(jnp.bfloat16),...]
    dot_general x7 -> x6, matrix products: 39.4 us -> 35.8 us  [contract_rows(): lax.dot_general(left, right, (((0,), (0,)), ((), ())), preferred_element_...]
  transfers between devices with their start and end apart: 13 -> 11, of which waited for: 10 -> 8; matrix products, arithmetic and copies ran while one was open for 10% -> 18% of each run, Pallas kernels for 0% -> 0%
where the time goes in v1:
time: 700 us; the launch traced here: 691 us
  waiting for transfers between devices  318 us (45%)
  matrix products  143 us (20%)
  blocking collectives  66.7 us (10%)
  Pallas kernels  53.5 us (8%)
  other arithmetic  52.8 us (8%)
  local copies, waits for them, and re-layouts  29.9 us (4%)
  between operations  15 us (2%)
  starting transfers between devices  12 us (2%)
    psum x1, waiting for transfers between devices, local(): lax.psum(grad_qkv_weight.astype(jnp.bfloat16), 'ep').astype(jnp.float32)  194 us
    reduce_scatter x4, waiting for transfers between devices, share_sum(): lax.psum_scatter(terms.astype(jnp.bfloat16), 'tp', scatter_dimension=2, t...  73.8 us
    pallas_call x1, Pallas kernels, forward(): pl.pallas_call(functools.partial(forward_kernel, n_tp, n_ep), out_shape=(...  53.5 us
    psum x1, blocking collectives, local(): lax.psum(grad_gain_one.astype(jnp.bfloat16), 'ep').astype(jnp.float32)  37.3 us
    dot_general x6, matrix products, contract_rows(): lax.dot_general(left, right, (((0,), (0,)), ((), ())), preferred_element_...  35.8 us
    all_to_all x1, blocking collectives, local(): lax.all_to_all(own_cols, 'ep', split_axis=0, concat_axis=0, tiled=True)  24.2 us
    all_gather x1, waiting for transfers between devices, fanout(): return lax.all_gather(piece, 'tp', axis=2, tiled=True)  23.2 us
    dot_general x5, matrix products, contract_cols(): lax.dot_general(left, right, (((1,), (1,)), ((), ())), preferred_element_...  22.2 us
  transfers between devices with their start and end apart: 11, of which 8 were waited for; matrix products, arithmetic and copies ran while one was open for 18% of the time, Pallas kernels for 0%

profile of v1, /device:TPU:0, one launch (start us, length us, event | category | flops | bytes accessed | tf_op | source)
XLA Modules:
  0.0 690.8 jit_solution(9088411176206679954)
XLA Ops:
  12.1 53.5 %attention_forward.1 = (bf16[3,1024,256]{2,1,0:T(8,128)(2,1)}, bf16[256,1024]{1,0:T(8,128)(2,1)}, f32[4,1024]{1,0:T(4,128)}, bf16[1024,1024]{1,0:T(8,128)(2,1)},...) custom-call(bf16[1024,1024]{1,0:T(8,128)(2,1)} %tok.1, ...), custom_call_target="tpu_custom_call" | custom-call | flops 8000000000 | bytes 30000000 | tf_op jit(solution)/shard_map/attention_forward/pallas_call | solution.py:267
  65.6 5.5 fusion.41
  71.2 24.2 %all_to_all.15 = bf16[8,192,256]{2,1,0:T(8,128)(2,1)} all-to-all(bf16[8,192,256]{2,1,0:T(8,128)(2,1)S(1)} %constant_dynamic-slice_fusion), channel_id=1, replica_groups=mesh['tp'=4,'ep'=8] {'ep'}, dimensions={0} | all-to-all | bytes 1572864 | tf_op jit(solution)/shard_map/all_to_all | solution.py:425
  95.5 3.9 fusion.104
  99.4 23.2 %all-gather.5.cloned.1.call-done = bf16[8,192,1024]{2,1,0:T(8,128)(2,1)} async-done(((bf16[8,192,256]{2,1,0:T(8,128)(2,1)}), bf16[8,192,1024]{2,1,0:T(8,128)(2,1)}) %all-gather.5.cloned.1.call-update) | async-done | bytes 3145744 | tf_op jit(solution)/shard_map/all_gather | solution.py:360
  122.7 3.0 fusion.108
  125.7 3.5 fusion.54
  129.3 7.5 %fusion.6 = bf16[1536,1024]{1,0:T(8,128)(2,1)S(1)} fusion(f32[1536,1024]{1,0:T(8,128)S(1)} %fusion.54, bf16[1,1024,1024]{2,1,0:T(8,128)(2,1)S(1)} %copy-done.37, bf16[1536,512]{1,0:T(8,128)(2,1)S(1)} %bitcast.161, bf16[1536,512]{1,0:T(8,128)(2,1)S(1)} %bitcast.159, f32[1536]{0:T(1024)S(1)} %divide_reduce_fusion), kind=kOutput, calls=%fused_computation.14 | convolution fusion | flops 3262119936 | bytes 14686208 | tf_op jit(solution)/shard_map/dot_general | solution.py:354
  136.9 4.9 convolution_convert_fusion
  142.7 4.7 fusion.109
  147.4 5.3 fusion.34
  154.1 3.7 convert_bitcast_fusion
  157.9 9.1 %convolution_convert_fusion.1 = bf16[1536,1024]{1,0:T(8,128)(2,1)} fusion(bf16[1,1024,1024]{2,1,0:T(8,128)(2,1)S(1)} %copy-done.38, f32[1536,1024]{1,0:T(8,128)} %copy-done.45), kind=kOutput, calls=%fused_computation.68 | convolution fusion | flops 3236954112 | bytes 11534336 | tf_op jit(solution)/shard_map/dot_general | solution.py:429
  167.1 6.9 convert_bitcast_fusion.1
  174.0 6.1 reduce-scatter.11.cloned.1.call-done
  180.0 5.5 all-to-all-start.2
  188.0 26.7 %reduce-scatter.9.cloned.1.call-done = bf16[1,1024,256]{2,1,0:T(8,128)(2,1)} async-done(((bf16[1,1024,1024]{2,1,0:T(8,128)(2,1)}), bf16[1,1024,256]{2,1,0:T(8,128)(2,1)}) %reduce-scatter.9.cloned.1.call-update) | async-done | bytes 524304 | tf_op jit(solution)/shard_map/reduce_scatter | solution.py:364
  214.7 3.3 fusion.73
  221.6 34.1 %reduce-scatter.7.cloned.1.call-done = bf16[8,192,256]{2,1,0:T(8,128)(2,1)} async-done(((bf16[8,192,1024]{2,1,0:T(8,128)(2,1)}), bf16[8,192,256]{2,1,0:T(8,128)(2,1)}) %reduce-scatter.7.cloned.1.call-update) | async-done | bytes 786448 | tf_op jit(solution)/shard_map/reduce_scatter | solution.py:364
  255.7 5.5 all-to-all-start.1
  261.3 4.1 convert_element_type.175
  265.4 2.8 copy.87
  272.4 5.5 fusion.92
  277.8 5.5 fusion.90
  283.3 7.0 %reduce-scatter.5.cloned.1.call-done = bf16[1,1024,256]{2,1,0:T(8,128)(2,1)} async-done(((bf16[1,1024,1024]{2,1,0:T(8,128)(2,1)}), bf16[1,1024,256]{2,1,0:T(8,128)(2,1)}) %reduce-scatter.5.cloned.1.call-update) | async-done | bytes 524304 | tf_op jit(solution)/shard_map/reduce_scatter | solution.py:364
  290.3 3.9 fusion.85
  294.2 5.2 all-gather
  302.8 12.3 %all-gather.9.cloned.1.call-done = bf16[1024,1024]{1,0:T(8,128)(2,1)} async-done(((bf16[1024,256]{1,0:T(8,128)(2,1)}), bf16[1024,1024]{1,0:T(8,128)(2,1)}) %all-gather.9.cloned.1.call-update) | async-done | bytes 2097168 | tf_op jit(solution)/shard_map/all_gather | solution.py:492
  315.2 6.5 multiply_reduce_fusion.2
  321.8 4.6 multiply_add_fusion
  328.4 5.4 multiply_reduce_fusion.1
  333.8 4.8 multiply_convert_fusion.1
  340.1 2.9 fusion.89
  345.3 5.6 multiply_reduce_fusion
  350.9 3.2 fusion.74
  356.2 7.1 %multiply_convert_fusion = bf16[4,512,1024]{2,1,0:T(8,128)(2,1)S(1)} fusion(f32[4,512,1024]{2,1,0:T(8,128)} %get-tuple-element.124, f32[4,512,1024]{2,1,0:T(8,128)} %fusion.92, f32[4,512]{1,0:T(4,128)S(1)} %get-tuple-element.123, f32[4,512]{1,0:T(4,128)S(1)} %get-tuple-element.112, pred[512,1024]{1,0:T(8,128)(4,1)} %get-tuple-element.114), kind=kLoop, calls=%fused_computation.2 | loop fusion | flops 12582912 | bytes 21512192 | tf_op jit(solution)/shard_map/convert_element_type | solution.py:532
  370.5 5.1 bitcast_convert_fusion
  378.7 6.1 convolution_convert_fusion.3
  384.8 4.4 convolution_convert_fusion.2
  390.8 3.3 fusion.65
  394.1 8.5 %convolution_bitcast_fusion.1 = f32[1,1024,1024]{2,1,0:T(8,128)} fusion(bf16[1536,1024]{1,0:T(8,128)(2,1)} %bitcast.143, bf16[1536,1024]{1,0:T(8,128)(2,1)} %copy-done.42), kind=kOutput, calls=%fused_computation.74 | convolution fusion | flops 3221225472 | bytes 10485760 | tf_op jit(solution)/shard_map/dot_general | solution.py:348
  402.6 9.8 %convolution_bitcast_fusion = f32[1,1024,1024]{2,1,0:T(8,128)} fusion(bf16[1536,512]{1,0:T(8,128)(2,1)S(1)} %bitcast.162, bf16[1536,512]{1,0:T(8,128)(2,1)S(1)} %bitcast.160, f32[1536]{0:T(1024)S(1)} %divide_reduce_fusion, f32[1536,1024]{1,0:T(8,128)} %copy-done.45), kind=kOutput, calls=%fused_computation.73 | convolution fusion | flops 3244818432 | bytes 13637632 | tf_op jit(solution)/shard_map/dot_general | solution.py:348
  413.5 13.6 %all-reduce.6.cloned.1.call-done = bf16[1024,1024]{1,0:T(8,128)(2,1)} async-done(((bf16[1024,1024]{1,0:T(8,128)(2,1)}), bf16[1024,1024]{1,0:T(8,128)(2,1)}) %all-reduce.6.cloned.1.call-update) | async-done | bytes 2097168 | tf_op jit(solution)/shard_map/psum | solution.py:562
  429.1 3.5 fusion.27
  432.5 37.3 %all-reduce.1 = (bf16[1024]{0:T(1024)(128)(2,1)S(1)}, bf16[1024]{0:T(1024)(128)(2,1)S(1)}, bf16[1024]{0:T(1024)(128)(2,1)S(1)}, bf16[1024]{0:T(1024)(128)(2,1)S(1)}, bf16[1024,2]{0,1:T(2,128)(2,1)S(1)}) all-reduce(bf16[1024]{0:T(1024)(128)(2,1)S(1)} %get-tuple-element.83, ...), channel_id=1, replica_groups=mesh['tp'=4,'ep'=8] {'ep'}, use_global_device_ids=true, to_apply=%region_22.23 | all-reduce | flops 6144 | bytes 24576 | tf_op jit(solution)/shard_map/psum | solution.py:573
  472.8 4.6 fusion.22
  477.5 194.4 %all-reduce.8.cloned.1.call-done = (bf16[3,1024,256]{1,2,0:T(8,128)(2,1)}, bf16[256,1024]{1,0:T(8,128)(2,1)}, bf16[1024,1024]{1,0:T(8,128)(2,1)}, bf16[1024,1024]{1,0:T(8,128)(2,1)}) async-done(((bf16[3,1024,256]{1,2,0:T(8,128)(2,1)}, bf16[256,1024]{1,0:T(8,128)(2,1)}, bf16[1024,1024]{1,0:T(8,128)(2,1)}, bf16[1024,1024]{1,0:T(8,128)(2,1)}), (bf16[3,1024,256]{1,2,0:T(8,128)(2,1)}, ...) | async-done | bytes 6291472 | tf_op jit(solution)/shard_map/psum | solution.py:568
  674.1 3.1 copy.95
  (181 shorter events, 55.6 us)
Async XLA Ops:
  7.2 118.5 %copy-start = (bf16[1,1024,1024]{2,1,0:T(8,128)(2,1)S(1)}, bf16[1,1024,1024]{2,1,0:T(8,128)(2,1)}, u32[]{:S(2)}) copy-start(bf16[1,1024,1024]{2,1,0:T(8,128)(2,1)} %param.29) | copy-start | bytes 6291460
  7.2 115.5 %all-gather.5.cloned.1.call-start = ((), (), s32[]{:S(2)}) async-start(), calls=%async_computation.8 | async-start | bytes 3932160 | tf_op jit(solution)/shard_map/all_gather | solution.py:360
  71.2 51.5 %copy-start.32 = (bf16[1024,2]{0,1:T(2,128)(2,1)S(1)}, bf16[1024,2]{0,1:T(2,128)(2,1)}, u32[]{:S(2)}) copy-start(bf16[1024,2]{0,1:T(2,128)(2,1)} %param.26) | copy-start | bytes 12292
  95.5 84.5 %reduce-scatter.11.cloned.1.call-start = ((), (), s32[]{:S(2)}) async-start(), calls=%async_computation.12 | async-start | bytes 3932160 | tf_op jit(solution)/shard_map/reduce_scatter | solution.py:364
  122.7 3.0 copy-start.7
  125.7 3.6 copy-start.21
  125.7 3.6 copy-start.23
  125.7 3.6 copy-start.37
  129.2 7.7 %copy-start.45 = (f32[1536,1024]{1,0:T(8,128)}, f32[1536,1024]{1,0:T(8,128)S(1)}, u32[]{:S(2)}) copy-start(f32[1536,1024]{1,0:T(8,128)S(1)} %fusion.54) | copy-start | bytes 18874372
  136.9 5.0 copy-start.42
  136.9 5.2 copy-start.8
  141.9 72.8 %reduce-scatter.9.cloned.1.call-start = ((), (), s32[]{:S(2)}) async-start(), calls=%async_computation.11 | async-start | bytes 2621440 | tf_op jit(solution)/shard_map/reduce_scatter | solution.py:364
  142.6 4.7 copy-start.9
  142.7 4.7 copy-start.39
  147.4 5.3 copy-start.43
  147.4 6.7 copy-start.36
  154.1 3.8 copy-start.38
  157.9 97.8 %reduce-scatter.7.cloned.1.call-start = ((), (), s32[]{:S(2)}) async-start(), calls=%async_computation.9 | async-start | bytes 3932160 | tf_op jit(solution)/shard_map/reduce_scatter | solution.py:364
  167.0 123.2 %reduce-scatter.5.cloned.1.call-start = ((), (), s32[]{:S(2)}) async-start(), calls=%async_computation.7 | async-start | bytes 2621440 | tf_op jit(solution)/shard_map/reduce_scatter | solution.py:364
  173.9 11.9 %copy-start.4 = (bf16[1024,1024]{1,0:T(8,128)(2,1)S(1)}, bf16[1024,1024]{1,0:T(8,128)(2,1)}, u32[]{:S(2)}) copy-start(bf16[1024,1024]{1,0:T(8,128)(2,1)} %tok.1) | copy-start | bytes 6291460
  173.9 40.8 %copy-start.41 = (s32[1,1024]{1,0:T(1,128)S(1)}, s32[1,1024]{1,0:T(1,128)}, u32[]{:S(2)}) copy-start(s32[1,1024]{1,0:T(1,128)} %get-tuple-element.24) | copy-start | bytes 12292
  180.0 34.7 %all-to-all-start.2 = ((bf16[8,192,256]{2,1,0:T(8,128)(2,1)}), bf16[8,192,256]{2,1,0:T(8,128)(2,1)}, u32[]{:S(2)}, u32[]{:S(2)}) async-start(bf16[8,192,256]{2,1,0:T(8,128)(2,1)} %reduce-scatter.11.cloned.1.call-done), calls=%async_computation.6 | async-start | bytes 1572864 | tf_op jit(solution)/shard_map/all_to_all | solution.py:370
  185.5 129.6 %all-gather.9.cloned.1.call-start = ((), (), s32[]{:S(2)}) async-start(), calls=%async_computation.13 | async-start | bytes 2621440 | tf_op jit(solution)/shard_map/all_gather | solution.py:492
  218.1 43.2 %copy-start.31 = (s32[1,1024]{1,0:T(1,128)S(1)}, s32[1,1024]{1,0:T(1,128)}, u32[]{:S(2)}) copy-start(s32[1,1024]{1,0:T(1,128)} %segr.1) | copy-start | bytes 12292
  255.7 34.6 %all-to-all-start.1 = ((bf16[8,192,256]{2,1,0:T(8,128)(2,1)}), bf16[8,192,256]{2,1,0:T(8,128)(2,1)}, u32[]{:S(2)}, u32[]{:S(2)}) async-start(bf16[8,192,256]{2,1,0:T(8,128)(2,1)} %reduce-scatter.7.cloned.1.call-done), calls=%async_computation.3 | async-start | bytes 1572864 | tf_op jit(solution)/shard_map/all_to_all | solution.py:370
  261.2 165.9 %all-reduce.6.cloned.1.call-start = ((), (), s32[]{:S(2)}) async-start(), calls=%async_computation.14 | async-start | bytes 4194304 | tf_op jit(solution)/shard_map/psum | solution.py:562
  290.3 24.9 %copy-start.35 = (f32[1024]{0:T(1024)S(1)}, f32[1024]{0:T(1024)}, u32[]{:S(2)}) copy-start(f32[1024]{0:T(1024)} %param.24) | copy-start | bytes 12292
  315.1 6.6 copy-start.5
  315.1 6.6 copy-start.10
  315.1 13.3 %slice-start.2 = ((s8[8388608]{0:T(1024)(128)(4,1)}), s8[4194304]{0:T(1024)(128)(4,1)S(1)}, s32[]{:S(2)}) async-start(s8[8388608]{0:T(1024)(128)(4,1)} %bitcast.136), calls=%async_computation.18 | async-start | bytes 8388608
  321.7 4.7 copy-start.25
  321.7 6.7 slice-start.3
  328.4 14.5 %slice-start = ((s8[8388608]{0:T(1024)(128)(4,1)}), s8[4194304]{0:T(1024)(128)(4,1)S(1)}, s32[]{:S(2)}) async-start(s8[8388608]{0:T(1024)(128)(4,1)} %bitcast.134), calls=%async_computation.16 | async-start | bytes 8388608
  333.8 9.1 %slice-start.1 = ((s8[8388608]{0:T(1024)(128)(4,1)}), s8[4194304]{0:T(1024)(128)(4,1)S(1)}, s32[]{:S(2)}) async-start(s8[8388608]{0:T(1024)(128)(4,1)} %bitcast.134), calls=%async_computation.17 | async-start | bytes 8388608
  340.0 2.9 copy-start.12
  370.5 5.2 copy-start.30
  375.6 101.9 %all-gather.7.cloned.1.call-start = ((), (), s32[]{:S(2)}) async-start(), calls=%async_computation.10 | async-start | bytes 2621440 | tf_op jit(solution)/shard_map/all_gather | solution.py:453
  378.4 293.5 %all-reduce.8.cloned.1.call-start = ((), (), s32[]{:S(2)}) async-start(), calls=%async_computation.15 | async-start | bytes 12582912 | tf_op jit(solution)/shard_map/psum | solution.py:568
  378.6 6.1 copy-start.11
  378.7 6.1 copy-start.44
  384.8 4.4 copy-start.3
  384.8 4.4 copy-start.26
  394.1 8.5 %copy-start.22 = (bf16[1,8,192,512]{3,2,1,0:T(8,128)(2,1)S(1)}, bf16[1,8,192,512]{3,2,1,0:T(8,128)(2,1)}, u32[]{:S(2)}) copy-start(bf16[1,8,192,512]{3,2,1,0:T(8,128)(2,1)} %get-tuple-element.106) | copy-start | bytes 4718596
  394.1 8.5 %copy-start.24 = (bf16[1,8,192,512]{3,2,1,0:T(8,128)(2,1)S(1)}, bf16[1,8,192,512]{3,2,1,0:T(8,128)(2,1)}, u32[]{:S(2)}) copy-start(bf16[1,8,192,512]{3,2,1,0:T(8,128)(2,1)} %get-tuple-element.107) | copy-start | bytes 4718596
  402.6 9.9 %copy-start.18 = (bf16[1024,1024]{1,0:T(8,128)(2,1)S(1)}, bf16[1024,1024]{1,0:T(8,128)(2,1)}, u32[]{:S(2)}) copy-start(bf16[1024,1024]{1,0:T(8,128)(2,1)} %get-tuple-element.23) | copy-start | bytes 6291460
  402.6 9.9 %copy-start.20 = (f32[1024,2]{1,0:T(8,128)S(1)}, f32[1024,2]{1,0:T(8,128)}, u32[]{:S(2)}) copy-start(f32[1024,2]{1,0:T(8,128)} %copy.85) | copy-start | bytes 24580
  671.8 5.3 copy-start.17
  679.7 4.1 copy-start.1
  (14 other events, 27.2 us)
Sparse Core Ops, SparseCore 0:
  95.6 27.0 all-gather.4
  142.0 37.9 reduce-scatter.10
  183.3 31.3 reduce-scatter.8
  217.7 37.9 reduce-scatter.6
  258.8 31.4 reduce-scatter.4
  292.3 22.8 all-gather.8
  375.7 51.3 all-reduce.5
  428.7 22.9 all-gather.6
  457.3 214.4 all-reduce.7
